TPU v7x, 768 devices: a whole 4x8x12 slice. The times are simulated.
768 devices in a mesh: row: 96 (over z, x, y_hi), col: 8 (over y_lo, core).
Axes of the slice: x: 4, y: 8 (y_hi: 2, y_lo: 4; y = y_hi * 4 + y_lo), z: 12, core: 2. Of those that a mesh axis runs over, the one named last changes fastest.
Arguments:
- vectors: float32 [393216, 16], P(('row', 'col')), may hold values from -6 to 6
- tiles: float32 [96, 8, 256, 64, 64], P('row', 'col'), may hold values from -0.125 to 0.125
- tile_rows: int32 [96, 8, 256], P('row', 'col'), may hold values from 0 to 63
- tile_cols: int32 [96, 8, 256], P('row', 'col'), may hold values from 0 to 767
- tile_count: int32 [96, 8], P('row', 'col'), may hold values from 1 to 256, as said below
Outputs:
- product: float32 [393216, 16], P(('row', 'col'))
Inputs may be any that keep to these rules, and one draw needn't show every extreme that they name: `tile_count`: device (0, c) has all 256 slots live; devices further along row hold fewer.
All inputs are finite; a program needn't handle non-finite values.
Results may differ from a plain program's by a relative error of at most 0.0001.
Values sent between devices are 32-bit elements; how exact they have to be, the bound alone decides.
No kernel may reach another device: no remote copies, remote signals or barrier semaphores. Data moves between devices by JAX's collectives and lax.ppermute only.
A program may use at most 64 MiB of HBM per device.

v0:
```python
import jax
import jax.numpy as jnp
from jax import lax
from jax.experimental import pallas as pl
from jax.experimental.pallas import tpu as pltpu
from jax.sharding import PartitionSpec as P

VEC = 16
TILE = 64
TPD = 256
S = 512
RT = 64
CT = 768
NZ, NX, NY = 12, 4, 2
NCOL = 8
PT = S // TILE
WIDE = VEC * TILE
CHUNK = CT // NX
GROUP = 4
LANES = 128
CHUNKS = 7
VMEM_LIMIT = 58 * 1024 * 1024


def row_index(z, x, y):
    return ((z % NZ) * NX + (x % NX)) * NY + (y % NY)


def row_shift(dx=0, dy=0):
    return [
        (row_index(z, x, y), row_index(z, x + dx, y + dy))
        for z in range(NZ)
        for x in range(NX)
        for y in range(NY)
    ]


Z_GROUPS = [[row_index(z, x, y) for z in range(NZ)] for x in range(NX) for y in range(NY)]
RING_GROUPS = [
    [row_index(z, x, y) * NCOL + c for y in range(NY) for c in range(NCOL)]
    for z in range(NZ)
    for x in range(NX)
]
XY_GROUPS = [[row_index(z, x, y) for x in range(NX) for y in range(NY)] for z in range(NZ)]


def three_parts(value):
    first = value.astype(jnp.bfloat16)
    rest = value - first.astype(jnp.float32)
    second = rest.astype(jnp.bfloat16)
    third = (rest - second.astype(jnp.float32)).astype(jnp.bfloat16)
    return first, second, third


def indicator(condition):
    return jnp.where(condition, 1.0, 0.0).astype(jnp.bfloat16)


def iota(shape, dim):
    return lax.broadcasted_iota(jnp.int32, shape, dim)


def put(halves, value):
    for half in range(TPD // LANES):
        halves[half] = value[:, half * LANES : (half + 1) * LANES]


def whole(halves):
    return jnp.concatenate([halves[half] for half in range(TPD // LANES)], axis=1)


def column(row):
    return jnp.broadcast_to(row, (8, row.shape[1])).T[:, :1]


def fetch(pairs, arrived):
    copies = [pltpu.make_async_copy(*pair, arrived.at[i]) for i, pair in enumerate(pairs)]
    for copy in copies:
        copy.start()
    return copies


def pick(picked, onehot, value):
    dims = (((0,), (0,)), ((), ()))
    put(
        picked,
        lax.dot_general(
            jnp.concatenate(three_parts(value)),
            jnp.concatenate([onehot] * 3),
            dims,
            preferred_element_type=jnp.float32,
        ),
    )


def place(onehot, value):
    return lax.dot_general(
        jnp.concatenate([onehot] * 3, axis=1),
        jnp.concatenate(three_parts(value), axis=1),
        (((1,), (1,)), ((), ())),
        preferred_element_type=jnp.float32,
    )


def backward_kernel(count, base, rows, rids_far, cids_far, far, out, side, rids, cids, tiles, arrived, picked, summed):
    own = rows.at[pl.ds(pl.multiple_of(base[0, 0], RT), RT)]
    copies = fetch([(own, side), (rids_far, rids), (cids_far, cids), (far, tiles)], arrived)
    for copy in copies[:3]:
        copy.wait()
    pick(picked, indicator(iota((RT, TPD), 0) == rids[...]), side[...])
    live = iota((1, TPD), 1) < count[0, 0]
    at_col = indicator((iota((CT, TPD), 0) == cids[...]) & live)
    copies[3].wait()
    for group in range(VEC // GROUP):
        for half in range(TPD // LANES):
            lanes = pl.ds(half * LANES, LANES)

            def step(a, totals):
                tile = tiles[a, :, lanes]
                return tuple(
                    total + tile * picked[half, pl.ds((group * GROUP + v) * TILE + a, 1), :]
                    for v, total in enumerate(totals)
                )

            zero = jnp.zeros((TILE, LANES), jnp.float32)
            totals = lax.fori_loop(0, TILE, step, (zero,) * GROUP, unroll=64)
            for v, total in enumerate(totals):
                summed[half, v * TILE : (v + 1) * TILE, :] = total
        out[:, group * GROUP * TILE : (group + 1) * GROUP * TILE] = place(at_col, whole(summed))


def forward_kernel(count, *refs):
    chunks, refs = refs[:CHUNKS], refs[CHUNKS:]
    places_far, rids_far, far, out, side, rids, places, tiles, arrived, picked, summed = refs
    pairs = [(places_far, places), (rids_far, rids)]
    start = 0
    for chunk in chunks:
        pairs.append((chunk, side.at[pl.ds(start, chunk.shape[0])]))
        start += chunk.shape[0]
    copies = fetch(pairs + [(far, tiles)], arrived)
    for copy in copies[:-1]:
        copy.wait()
    pick(picked, indicator(iota((CT, TPD), 0) == places[...]), side[...])
    live = iota((1, TPD), 1) < count[0, 0]
    at_row = indicator((iota((RT, TPD), 0) == rids[...]) & live)
    copies[-1].wait()
    for group in range(VEC // GROUP):
        for half in range(TPD // LANES):
            lanes = pl.ds(half * LANES, LANES)
            blocks = [
                picked[half, (group * GROUP + v) * TILE : (group * GROUP + v + 1) * TILE, :]
                for v in range(GROUP)
            ]

            def step(a, carry):
                tile = tiles[a, :, lanes]
                for v, block in enumerate(blocks):
                    summed[half, pl.ds(v * TILE + a, 1), :] = jnp.sum(
                        tile * block, axis=0, keepdims=True
                    )
                return carry

            lax.fori_loop(0, TILE, step, 0, unroll=64)
        out[:, group * GROUP * TILE : (group + 1) * GROUP * TILE] = place(at_row, whole(summed))


def run(kernel, rows, side, scalars, *operands):
    return pl.pallas_call(
        kernel,
        out_shape=jax.ShapeDtypeStruct((rows, WIDE), jnp.float32),
        in_specs=[pl.BlockSpec(memory_space=pltpu.SMEM)] * len(scalars)
        + [pl.BlockSpec(memory_space=pltpu.HBM)] * len(operands),
        out_specs=pl.BlockSpec(memory_space=pltpu.VMEM),
        scratch_shapes=[
            pltpu.VMEM((side, WIDE), jnp.float32),
            pltpu.VMEM((1, TPD), jnp.int32),
            pltpu.VMEM((1, TPD), jnp.int32),
            pltpu.VMEM((TILE, TILE, TPD), jnp.float32),
            pltpu.SemaphoreType.DMA((len(operands),)),
            pltpu.VMEM((TPD // LANES, WIDE, LANES), jnp.float32),
            pltpu.VMEM((TPD // LANES, GROUP * TILE, LANES), jnp.float32),
        ],
        compiler_params=pltpu.CompilerParams(vmem_limit_bytes=VMEM_LIMIT),
        cost_estimate=pl.CostEstimate(
            flops=10_000_000_000, bytes_accessed=8 * 1024 * 1024, transcendentals=0
        ),
    )(*scalars, *operands)


def local(vectors, tiles, tile_rows, tile_cols, tile_count):
    me, me_col = lax.axis_index("row"), lax.axis_index("col")
    my_x, my_y = (me >> 1) & 3, me & 1
    piece = vectors.T.reshape(VEC, PT, TILE).transpose(1, 0, 2).reshape(PT, WIDE)
    block = tiles[0, 0].transpose(1, 2, 0)
    rids, cids = tile_rows[0], tile_cols[0]

    rows = lax.all_gather(
        piece, ("row", "col"), axis_index_groups=RING_GROUPS, axis=0, tiled=True
    )
    base = (my_y * RT).reshape(1, 1)
    col_part = run(backward_kernel, CT, RT, (tile_count, base), rows, rids, cids, block)
    col_sum = lax.psum_scatter(
        col_part, "row", axis_index_groups=Z_GROUPS, scatter_dimension=0, tiled=True
    )

    mine = lax.all_gather(
        lax.dynamic_slice_in_dim(rows.reshape(NY, -1, WIDE), me_col * PT, PT, 1).reshape(-1, WIDE),
        "row",
        axis_index_groups=Z_GROUPS,
        axis=0,
        tiled=True,
    )
    first, second = mine[: CHUNK // 2], mine[CHUNK // 2 :]
    left_first = lax.ppermute(first, "row", row_shift(dx=1))
    right_second = lax.ppermute(second, "row", row_shift(dx=-1))
    left_second = lax.ppermute(second, "row", row_shift(dx=1))
    right_first = lax.ppermute(first, "row", row_shift(dx=-1))
    far_first = lax.ppermute(left_first, "row", row_shift(dx=1))
    far_second = lax.ppermute(right_second, "row", row_shift(dx=-1))
    chunks = [mine, left_first, left_second, far_first, far_second, right_first, right_second]
    z, x, y, rest = cids >> 6, (cids >> 4) & 3, (cids >> 3) & 1, cids & 7
    places = ((my_x - x) & 3) * CHUNK + (z * NY + y) * PT + rest
    places, col_sum = lax.optimization_barrier((places, col_sum))
    col_terms = lax.all_to_all(
        col_sum, "row", 0, 0, axis_index_groups=XY_GROUPS, tiled=True
    ).reshape(NX * NY, PT, WIDE)
    row_part = run(forward_kernel, RT, CT, (tile_count,), *chunks, places, rids, block)
    row_terms = lax.all_to_all(row_part, "col", 0, 0, tiled=True).reshape(-1, PT, WIDE)
    total = col_terms.sum(axis=0) + row_terms.sum(axis=0)
    return total.reshape(PT, VEC, TILE).transpose(1, 0, 2).reshape(VEC, S).T


def solution(mesh):
    placed = (
        P(("row", "col"), None),
        P("row", "col", None, None, None),
        P("row", "col", None),
        P("row", "col", None),
        P("row", "col"),
    )
    return jax.shard_map(
        local, mesh=mesh, in_specs=placed, out_specs=P(("row", "col"), None), check_vma=False
    )
```

profile of v0, /device:TPU:57, one launch (start us, length us, event | category | flops | bytes accessed | tf_op | source)
XLA Modules:
  0.0 150.8 jit_solution(4184129676692958877)
XLA Ops:
  6.5 0.0 reduce-scatter.2.cloned.1.call-start
  7.2 0.8 reshape.119
  8.0 0.1 reshape.120
  8.1 25.0 %all_gather.6.rows = f32[128,1024]{1,0:T(8,128)} all-gather(f32[8,1024]{1,0:T(8,128)S(1)} %reshape.120), channel_id=1, replica_groups={{0,1,2,3,4,5,6,7,8,9,10,11,12,13,14,15},{16,17,18,19,20,21,22,23,24,25,..., dimensions={0}, use_global_device_ids=true | all-gather | bytes 557056 | tf_op jit(solution)/shard_map/all_gather | solution.py:197
  33.1 9.8 %shard_map.55 = f32[768,1024]{1,0:T(8,128)} custom-call(s32[1,1]{1,0:T(1,128)S(6)} %copy.12.count, s32[1,1]{1,0:T(1,128)} %bitcast.1.base, f32[128,1024]{1,0:T(8,128)} %all_gather.6.rows, s32[1,256]{1,0:T(1,128)} %bitcast.27, s32[1,256]{1,0:T(1,128)} %bitcast.24, f32[64,64,256]{2,1,0:T(8,128)} %bitcast.25), custom_call_target="tpu_custom_call" | custom-call | flops 10000000000 | bytes 8388608 | tf_op jit(solution)/shard_map/pallas_call | solution.py:168
  43.0 0.0 copy-start.1
  43.0 0.0 reduce-scatter.2.cloned.1.call-update
  43.0 0.8 dynamic-slice_bitcast_fusion
  43.9 27.6 %all_gather.7.refs_0_ = f32[192,1024]{1,0:T(8,128)S(1)} all-gather(f32[16,1024]{1,0:T(8,128)S(1)} %dynamic-slice_bitcast_fusion), channel_id=1, replica_groups={{0,64,128,192,256,320,384,448,512,576,640,704},{8,72,136,200,264,328,39..., dimensions={0}, use_global_device_ids=true | all-gather | bytes 851968 | tf_op jit(solution)/shard_map/all_gather | solution.py:206
  71.5 0.0 copy-start
  71.5 0.1 fusion
  71.5 3.1 %collective-permute-start = (f32[96,1024]{1,0:T(8,128)S(1)}, f32[96,1024]{1,0:T(8,128)S(1)}, u32[]{:S(2)}, u32[]{:S(2)}) collective-permute-start(f32[96,1024]{1,0:T(8,128)S(1)} %get-tuple-element.10), channel_id=1, source_target_pairs={{0,16},{8,24},{16,32},{24,40},{32,48},{40,56},{48,0},{56,8},{64,80... | collective-permute-start | bytes 1179656 | tf_op jit(solution)/shard_map/ppermute | solution.py:214
  74.6 3.4 %collective-permute-start.3 = (f32[96,1024]{1,0:T(8,128)S(1)}, f32[96,1024]{1,0:T(8,128)S(1)}, u32[]{:S(2)}, u32[]{:S(2)}) collective-permute-start(f32[96,1024]{1,0:T(8,128)S(1)} %get-tuple-element.9), channel_id=1, source_target_pairs={{0,48},{8,56},{16,0},{24,8},{32,16},{40,24},{48,32},{56,40},{64,11... | collective-permute-start | bytes 1179656 | tf_op jit(solution)/shard_map/ppermute | solution.py:215
  78.0 1.9 %collective-permute-start.1 = (f32[96,1024]{1,0:T(8,128)S(1)}, f32[96,1024]{1,0:T(8,128)S(1)}, u32[]{:S(2)}, u32[]{:S(2)}) collective-permute-start(f32[96,1024]{1,0:T(8,128)S(1)} %get-tuple-element.9), channel_id=1, source_target_pairs={{0,16},{8,24},{16,32},{24,40},{32,48},{40,56},{48,0},{56,8},{64,80... | collective-permute-start | bytes 1179656 | tf_op jit(solution)/shard_map/ppermute | solution.py:216
  80.0 4.6 %collective-permute-start.5 = (f32[96,1024]{1,0:T(8,128)S(1)}, f32[96,1024]{1,0:T(8,128)S(1)}, u32[]{:S(2)}, u32[]{:S(2)}) collective-permute-start(f32[96,1024]{1,0:T(8,128)S(1)} %get-tuple-element.10), channel_id=1, source_target_pairs={{0,48},{8,56},{16,0},{24,8},{32,16},{40,24},{48,32},{56,40},{64,11... | collective-permute-start | bytes 1179656 | tf_op jit(solution)/shard_map/ppermute | solution.py:217
  84.6 0.0 collective-permute-done.refs_1_
  84.6 0.0 copy-start.2
  84.6 1.9 %collective-permute-start.2 = (f32[96,1024]{1,0:T(8,128)S(1)}, f32[96,1024]{1,0:T(8,128)}, u32[]{:S(2)}, u32[]{:S(2)}) collective-permute-start(f32[96,1024]{1,0:T(8,128)S(1)} %collective-permute-done.refs_1_), channel_id=1, source_target_pairs={{0,16},{8,24},{16,32},{24,40},{32,48},{40,56},{48,0},{56,8},{64,80... | collective-permute-start | bytes 1179656 | tf_op jit(solution)/shard_map/ppermute | solution.py:218
  86.5 0.0 collective-permute-done.3.refs_6_
  86.5 0.0 copy-start.3
  86.5 4.6 %collective-permute-start.4 = (f32[96,1024]{1,0:T(8,128)S(1)}, f32[96,1024]{1,0:T(8,128)}, u32[]{:S(2)}, u32[]{:S(2)}) collective-permute-start(f32[96,1024]{1,0:T(8,128)S(1)} %collective-permute-done.3.refs_6_), channel_id=1, source_target_pairs={{0,48},{8,56},{16,0},{24,8},{32,16},{40,24},{48,32},{56,40},{64,11... | collective-permute-start | bytes 1179656 | tf_op jit(solution)/shard_map/ppermute | solution.py:219
  91.1 0.0 copy-done.1
  91.1 0.6 and_add_fusion.refs_7_
  91.7 9.7 %reduce-scatter.2.cloned.1.call-done = f32[64,1024]{1,0:T(8,128)} async-done(((f32[768,1024]{1,0:T(8,128)}), f32[64,1024]{1,0:T(8,128)}) %reduce-scatter.2.cloned.1.call-update) | async-done | bytes 262160 | tf_op jit(solution)/shard_map/reduce_scatter | solution.py:202
  101.4 9.1 %all-to-all-start = ((f32[8,8,1024]{2,1,0:T(8,128)}), f32[8,8,1024]{2,1,0:T(8,128)S(1)}, u32[]{:S(2)}, u32[]{:S(2)}) async-start(f32[8,8,1024]{2,1,0:T(8,128)} %bitcast.19), calls=%async_computation.1 | async-start | bytes 524288 | tf_op jit(solution)/shard_map/all_to_all | solution.py:224
  110.5 0.0 collective-permute-done.1.refs_2_
  110.5 0.0 copy-start.4
  110.5 0.0 collective-permute-done.5.refs_5_
  110.5 0.0 copy-start.5
  110.5 0.0 collective-permute-done.2.refs_3_
  110.5 0.0 collective-permute-done.4.refs_4_
  110.5 0.0 copy-done
  110.6 0.0 copy-done.2
  110.6 0.0 copy-done.3
  110.6 0.7 copy-done.4
  111.2 0.1 copy-done.5
  111.4 10.9 %shard_map.56 = f32[64,1024]{1,0:T(8,128)} custom-call(s32[1,1]{1,0:T(1,128)S(6)} %copy.12.count, f32[192,1024]{1,0:T(8,128)} %copy-done, f32[96,1024]{1,0:T(8,128)} %copy-done.2, f32[96,1024]{1,0:T(8,128)} %copy-done.4, f32[96,1024]{1,0:T(8,128)} %collective-permute-done.2.refs_3_, f32[96,1024]{1,0:T(8,128)} %collective-permute-done.4.refs_4_, ...), custom_call_target="tpu_custom_call" | custom-call | flops 10000000000 | bytes 8388608 | tf_op jit(solution)/shard_map/pallas_call | solution.py:168
  122.3 0.0 all-to-all-done
  122.3 13.7 %all-to-all-start.1 = ((f32[8,8,1024]{2,1,0:T(8,128)}), f32[8,8,1024]{2,1,0:T(8,128)S(1)}, u32[]{:S(2)}, u32[]{:S(2)}) async-start(f32[8,8,1024]{2,1,0:T(8,128)} %bitcast.20), calls=%async_computation.2 | async-start | bytes 524288 | tf_op jit(solution)/shard_map/all_to_all | solution.py:228
  136.0 7.0 %all-to-all-done.1 = f32[8,8,1024]{2,1,0:T(8,128)S(1)} async-done(((f32[8,8,1024]{2,1,0:T(8,128)}), f32[8,8,1024]{2,1,0:T(8,128)S(1)}, u32[]{:S(2)}, u32[]{:S(2)}) %all-to-all-start.1) | async-done | bytes 262176 | tf_op jit(solution)/shard_map/all_to_all | solution.py:228
  143.1 0.1 add.50
  143.2 0.7 reshape.123
  (5 shorter events, 0.1 us)
Async XLA Ops:
  6.5 94.9 %reduce-scatter.2.cloned.1.call-start = ((), (), s32[]{:S(2)}) async-start(), calls=%async_computation.3 | async-start | bytes 3407872 | tf_op jit(solution)/shard_map/reduce_scatter | solution.py:202
  43.0 48.1 %copy-start.1 = (s32[1,1,256]{2,1,0:T(1,128)S(1)}, s32[1,1,256]{2,1,0:T(1,128)}, u32[]{:S(2)}) copy-start(s32[1,1,256]{2,1,0:T(1,128)} %param.8) | copy-start | bytes 3076
  71.5 39.1 %copy-start = (f32[192,1024]{1,0:T(8,128)}, f32[192,1024]{1,0:T(8,128)S(1)}, u32[]{:S(2)}) copy-start(f32[192,1024]{1,0:T(8,128)S(1)} %all_gather.7.refs_0_) | copy-start | bytes 2359300
  71.5 13.0 %collective-permute-start = (f32[96,1024]{1,0:T(8,128)S(1)}, f32[96,1024]{1,0:T(8,128)S(1)}, u32[]{:S(2)}, u32[]{:S(2)}) collective-permute-start(f32[96,1024]{1,0:T(8,128)S(1)} %get-tuple-element.10), channel_id=1, source_target_pairs={{0,16},{8,24},{16,32},{24,40},{32,48},{40,56},{48,0},{56,8},{64,80... | collective-permute-start | bytes 1179656 | tf_op jit(solution)/shard_map/ppermute | solution.py:214
  74.6 11.9 %collective-permute-start.3 = (f32[96,1024]{1,0:T(8,128)S(1)}, f32[96,1024]{1,0:T(8,128)S(1)}, u32[]{:S(2)}, u32[]{:S(2)}) collective-permute-start(f32[96,1024]{1,0:T(8,128)S(1)} %get-tuple-element.9), channel_id=1, source_target_pairs={{0,48},{8,56},{16,0},{24,8},{32,16},{40,24},{48,32},{56,40},{64,11... | collective-permute-start | bytes 1179656 | tf_op jit(solution)/shard_map/ppermute | solution.py:215
  78.0 32.5 %collective-permute-start.1 = (f32[96,1024]{1,0:T(8,128)S(1)}, f32[96,1024]{1,0:T(8,128)S(1)}, u32[]{:S(2)}, u32[]{:S(2)}) collective-permute-start(f32[96,1024]{1,0:T(8,128)S(1)} %get-tuple-element.9), channel_id=1, source_target_pairs={{0,16},{8,24},{16,32},{24,40},{32,48},{40,56},{48,0},{56,8},{64,80... | collective-permute-start | bytes 1179656 | tf_op jit(solution)/shard_map/ppermute | solution.py:216
  80.0 30.5 %collective-permute-start.5 = (f32[96,1024]{1,0:T(8,128)S(1)}, f32[96,1024]{1,0:T(8,128)S(1)}, u32[]{:S(2)}, u32[]{:S(2)}) collective-permute-start(f32[96,1024]{1,0:T(8,128)S(1)} %get-tuple-element.10), channel_id=1, source_target_pairs={{0,48},{8,56},{16,0},{24,8},{32,16},{40,24},{48,32},{56,40},{64,11... | collective-permute-start | bytes 1179656 | tf_op jit(solution)/shard_map/ppermute | solution.py:217
  84.6 26.0 %copy-start.2 = (f32[96,1024]{1,0:T(8,128)}, f32[96,1024]{1,0:T(8,128)S(1)}, u32[]{:S(2)}) copy-start(f32[96,1024]{1,0:T(8,128)S(1)} %collective-permute-done.refs_1_) | copy-start | bytes 1179652
  84.6 26.0 %collective-permute-start.2 = (f32[96,1024]{1,0:T(8,128)S(1)}, f32[96,1024]{1,0:T(8,128)}, u32[]{:S(2)}, u32[]{:S(2)}) collective-permute-start(f32[96,1024]{1,0:T(8,128)S(1)} %collective-permute-done.refs_1_), channel_id=1, source_target_pairs={{0,16},{8,24},{16,32},{24,40},{32,48},{40,56},{48,0},{56,8},{64,80... | collective-permute-start | bytes 1179656 | tf_op jit(solution)/shard_map/ppermute | solution.py:218
  86.5 24.1 %copy-start.3 = (f32[96,1024]{1,0:T(8,128)}, f32[96,1024]{1,0:T(8,128)S(1)}, u32[]{:S(2)}) copy-start(f32[96,1024]{1,0:T(8,128)S(1)} %collective-permute-done.3.refs_6_) | copy-start | bytes 1179652
  86.5 24.0 %collective-permute-start.4 = (f32[96,1024]{1,0:T(8,128)S(1)}, f32[96,1024]{1,0:T(8,128)}, u32[]{:S(2)}, u32[]{:S(2)}) collective-permute-start(f32[96,1024]{1,0:T(8,128)S(1)} %collective-permute-done.3.refs_6_), channel_id=1, source_target_pairs={{0,48},{8,56},{16,0},{24,8},{32,16},{40,24},{48,32},{56,40},{64,11... | collective-permute-start | bytes 1179656 | tf_op jit(solution)/shard_map/ppermute | solution.py:219
  101.4 20.9 %all-to-all-start = ((f32[8,8,1024]{2,1,0:T(8,128)}), f32[8,8,1024]{2,1,0:T(8,128)S(1)}, u32[]{:S(2)}, u32[]{:S(2)}) async-start(f32[8,8,1024]{2,1,0:T(8,128)} %bitcast.19), calls=%async_computation.1 | async-start | bytes 524288 | tf_op jit(solution)/shard_map/all_to_all | solution.py:224
  110.5 0.7 copy-start.4
  110.5 0.9 copy-start.5
  122.3 20.8 %all-to-all-start.1 = ((f32[8,8,1024]{2,1,0:T(8,128)}), f32[8,8,1024]{2,1,0:T(8,128)S(1)}, u32[]{:S(2)}, u32[]{:S(2)}) async-start(f32[8,8,1024]{2,1,0:T(8,128)} %bitcast.20), calls=%async_computation.2 | async-start | bytes 524288 | tf_op jit(solution)/shard_map/all_to_all | solution.py:228
Sparse Core Ops, SparseCore 0:
  43.1 58.2 reduce-scatter.1
where the time goes:
time: 151 us
  blocking collectives  52.6 us (35%)
  starting transfers between devices  42.3 us (28%)
  Pallas kernels  20.7 us (14%)
  waiting for transfers between devices  16.8 us (11%)
  between operations  14.3 us (9%)
  local copies, waits for them, and re-layouts  3.48 us (2%)
    all_gather x1, blocking collectives, local(): lax.all_gather(lax.dynamic_slice_in_dim(rows.reshape(NY, -1, WIDE), me_co...  27.6 us
    all_gather x1, blocking collectives, local(): lax.all_gather(piece, ('row', 'col'), axis_index_groups=RING_GROUPS, axis...  25 us
    pallas_call x2, Pallas kernels, run(): pl.pallas_call(kernel, out_shape=jax.ShapeDtypeStruct((rows, WIDE), jnp.f...  20.7 us
    all_to_all x1, starting transfers between devices, local(): lax.all_to_all(row_part, 'col', 0, 0, tiled=True).reshape(-1, PT, WIDE)  13.7 us
    reduce_scatter x1, waiting for transfers between devices, local(): lax.psum_scatter(col_part, 'row', axis_index_groups=Z_GROUPS, scatter_dim...  9.7 us
    all_to_all x1, starting transfers between devices, local(): lax.all_to_all(col_sum, 'row', 0, 0, axis_index_groups=XY_GROUPS, tiled=T...  9.11 us
    all_to_all x1, waiting for transfers between devices, local(): lax.all_to_all(row_part, 'col', 0, 0, tiled=True).reshape(-1, PT, WIDE)  7.04 us
    ppermute x1, starting transfers between devices, local(): far_second = lax.ppermute(right_second, 'row', row_shift(dx=-1))  4.57 us
  transfers between devices with their start and end apart: 9, of which 2 were waited for; matrix products, arithmetic and copies ran while one was open for 1% of the time, Pallas kernels for 7%

commit v1 on v0

--- a/solution.py
+++ b/solution.py
@@ -12,7 +12,7 @@
 RT = 64
 CT = 768
 NZ, NX, NY = 12, 4, 2
-NCOL = 8
+NCOL, NYL = 8, 4
 PT = S // TILE
 WIDE = VEC * TILE
 CHUNK = CT // NX
@@ -24,6 +24,12 @@
 
 def row_index(z, x, y):
     return ((z % NZ) * NX + (x % NX)) * NY + (y % NY)
+
+
+def col_shift(dy=0, core=0):
+    return [
+        (y * 2 + k, ((y + dy) % NYL) * 2 + (k ^ core)) for y in range(NYL) for k in range(2)
+    ]
 
 
 def row_shift(dx=0, dy=0):
@@ -129,10 +135,10 @@
         out[:, group * GROUP * TILE : (group + 1) * GROUP * TILE] = place(at_col, whole(summed))
 
 
-def forward_kernel(count, *refs):
+def forward_kernel(count, row, col, *refs):
     chunks, refs = refs[:CHUNKS], refs[CHUNKS:]
-    places_far, rids_far, far, out, side, rids, places, tiles, arrived, picked, summed = refs
-    pairs = [(places_far, places), (rids_far, rids)]
+    cids_far, rids_far, far, own, mate, side, rids, cids, tiles, arrived, picked, summed = refs
+    pairs = [(cids_far, cids), (rids_far, rids)]
     start = 0
     for chunk in chunks:
         pairs.append((chunk, side.at[pl.ds(start, chunk.shape[0])]))
@@ -140,9 +146,15 @@
     copies = fetch(pairs + [(far, tiles)], arrived)
     for copy in copies[:-1]:
         copy.wait()
-    pick(picked, indicator(iota((CT, TPD), 0) == places[...]), side[...])
+    tile = cids[...]
+    x, rest = (tile >> 4) & 3, (tile >> 6) * (NY * PT) + (tile & 15)
+    places = (((row[0, 0] >> 1) - x) & 3) * CHUNK + rest
+    pick(picked, indicator(iota((CT, TPD), 0) == places), side[...])
+    tile, me = rids[...], col[0, 0]
+    core, y = ((tile >> 3) ^ me) & 1, ((tile >> 4) - (me >> 1)) & 3
+    places = core * (RT // 2) + y * PT + (tile & 7)
     live = iota((1, TPD), 1) < count[0, 0]
-    at_row = indicator((iota((RT, TPD), 0) == rids[...]) & live)
+    at_row = indicator((iota((RT, TPD), 0) == places) & live)
     copies[-1].wait()
     for group in range(VEC // GROUP):
         for half in range(TPD // LANES):
@@ -161,16 +173,18 @@
                 return carry
 
             lax.fori_loop(0, TILE, step, 0, unroll=64)
-        out[:, group * GROUP * TILE : (group + 1) * GROUP * TILE] = place(at_row, whole(summed))
-
-
-def run(kernel, rows, side, scalars, *operands):
+        columns = slice(group * GROUP * TILE, (group + 1) * GROUP * TILE)
+        sums = place(at_row, whole(summed))
+        own[:, columns], mate[:, columns] = sums[: RT // 2], sums[RT // 2 :]
+
+
+def run(kernel, outs, side, scalars, *operands):
     return pl.pallas_call(
         kernel,
-        out_shape=jax.ShapeDtypeStruct((rows, WIDE), jnp.float32),
+        out_shape=[jax.ShapeDtypeStruct((rows, WIDE), jnp.float32) for rows in outs],
         in_specs=[pl.BlockSpec(memory_space=pltpu.SMEM)] * len(scalars)
         + [pl.BlockSpec(memory_space=pltpu.HBM)] * len(operands),
-        out_specs=pl.BlockSpec(memory_space=pltpu.VMEM),
+        out_specs=[pl.BlockSpec(memory_space=pltpu.VMEM)] * len(outs),
         scratch_shapes=[
             pltpu.VMEM((side, WIDE), jnp.float32),
             pltpu.VMEM((1, TPD), jnp.int32),
@@ -198,7 +212,7 @@
         piece, ("row", "col"), axis_index_groups=RING_GROUPS, axis=0, tiled=True
     )
     base = (my_y * RT).reshape(1, 1)
-    col_part = run(backward_kernel, CT, RT, (tile_count, base), rows, rids, cids, block)
+    (col_part,) = run(backward_kernel, [CT], RT, (tile_count, base), rows, rids, cids, block)
     col_sum = lax.psum_scatter(
         col_part, "row", axis_index_groups=Z_GROUPS, scatter_dimension=0, tiled=True
     )
@@ -218,15 +232,27 @@
     far_first = lax.ppermute(left_first, "row", row_shift(dx=1))
     far_second = lax.ppermute(right_second, "row", row_shift(dx=-1))
     chunks = [mine, left_first, left_second, far_first, far_second, right_first, right_second]
-    z, x, y, rest = cids >> 6, (cids >> 4) & 3, (cids >> 3) & 1, cids & 7
-    places = ((my_x - x) & 3) * CHUNK + (z * NY + y) * PT + rest
-    places, col_sum = lax.optimization_barrier((places, col_sum))
+    own, others = run(
+        forward_kernel,
+        [RT // 2, RT // 2],
+        CT,
+        (tile_count, me.reshape(1, 1), me_col.reshape(1, 1)),
+        *chunks,
+        cids,
+        rids,
+        block,
+    )
+
+    own, col_sum = lax.optimization_barrier((own, col_sum))
     col_terms = lax.all_to_all(
         col_sum, "row", 0, 0, axis_index_groups=XY_GROUPS, tiled=True
     ).reshape(NX * NY, PT, WIDE)
-    row_part = run(forward_kernel, RT, CT, (tile_count,), *chunks, places, rids, block)
-    row_terms = lax.all_to_all(row_part, "col", 0, 0, tiled=True).reshape(-1, PT, WIDE)
-    total = col_terms.sum(axis=0) + row_terms.sum(axis=0)
+    mate = lax.ppermute(others, "col", col_shift(core=1))
+    pair = (own + mate).reshape(NYL, PT, WIDE)
+    row_total = pair[0]
+    for d in range(1, NYL):
+        row_total = row_total + lax.ppermute(pair[d], "col", col_shift(dy=d))
+    total = col_terms.sum(axis=0) + row_total
     return total.reshape(PT, VEC, TILE).transpose(1, 0, 2).reshape(VEC, S).T
 
 

time: 151 us -> 155 us (1.026); the launches traced: 151 us -> 153 us
    ppermute x0 -> x4, starting transfers between devices: none -> 16.9 us  [the longest x3 9.22 us: local(): row_total = row_total + lax.ppermute(pair[d], 'col', col_shift(dy=d))]
    all_to_all x1 -> x0, starting transfers between devices: 13.7 us -> none  [local(): lax.all_to_all(row_part, 'col', 0, 0, tiled=True).reshape(-1, PT, WIDE)]
    reduce_scatter x1, waiting for transfers between devices: 9.7 us -> 0.02 us  [local(): lax.psum_scatter(col_part, 'row', axis_index_groups=Z_GROUPS, scatter_dim...]
    ppermute x1, waiting for transfers between devices: 0.01 us -> 7.55 us  [local(): far_second = lax.ppermute(right_second, 'row', row_shift(dx=-1))]
    all_to_all x1 -> x0, waiting for transfers between devices: 7.04 us -> none  [local(): lax.all_to_all(row_part, 'col', 0, 0, tiled=True).reshape(-1, PT, WIDE)]
    ppermute x0 -> x4, waiting for transfers between devices: none -> 4.85 us  [the longest x3 3.68 us: local(): row_total = row_total + lax.ppermute(pair[d], 'col', col_shift(dy=d))]
    ppermute x1, waiting for transfers between devices: 0.01 us -> 2.58 us  [local(): right_first = lax.ppermute(first, 'row', row_shift(dx=-1))]
  transfers between devices with their start and end apart: 9 -> 12, of which waited for: 2 -> 7; matrix products, arithmetic and copies ran while one was open for 1% -> 1% of each run, Pallas kernels for 7% -> 7%
where the time goes in v1:
time: 155 us; the launch traced here: 153 us
  blocking collectives  52.6 us (34%)
  starting transfers between devices  43.7 us (28%)
  Pallas kernels  20.8 us (13%)
  waiting for transfers between devices  17.1 us (11%)
  between operations  14.3 us (9%)
  local copies, waits for them, and re-layouts  3.37 us (2%)
    all_gather x1, blocking collectives, local(): lax.all_gather(lax.dynamic_slice_in_dim(rows.reshape(NY, -1, WIDE), me_co...  27.6 us
    all_gather x1, blocking collectives, local(): lax.all_gather(piece, ('row', 'col'), axis_index_groups=RING_GROUPS, axis...  25 us
    pallas_call x2, Pallas kernels, run(): pl.pallas_call(kernel, out_shape=[jax.ShapeDtypeStruct((rows, WIDE), jnp....  20.8 us
    ppermute x3, starting transfers between devices, local(): row_total = row_total + lax.ppermute(pair[d], 'col', col_shift(dy=d))  9.22 us
    all_to_all x1, starting transfers between devices, local(): lax.all_to_all(col_sum, 'row', 0, 0, axis_index_groups=XY_GROUPS, tiled=T...  8.53 us
    ppermute x1, starting transfers between devices, local(): mate = lax.ppermute(others, 'col', col_shift(core=1))  7.72 us
    ppermute x1, waiting for transfers between devices, local(): far_second = lax.ppermute(right_second, 'row', row_shift(dx=-1))  7.55 us
    ppermute x1, starting transfers between devices, local(): right_first = lax.ppermute(first, 'row', row_shift(dx=-1))  4.37 us
  transfers between devices with their start and end apart: 12, of which 7 were waited for; matrix products, arithmetic and copies ran while one was open for 1% of the time, Pallas kernels for 7%

profile of v1, /device:TPU:57, one launch (start us, length us, event | category | flops | bytes accessed | tf_op | source)
XLA Modules:
  0.0 152.8 jit_solution(16445614412163600547)
XLA Ops:
  6.5 0.0 reduce-scatter.2.cloned.1.call-start
  7.2 0.8 reshape.42
  8.0 0.1 reshape.43
  8.1 25.0 %all_gather.6.rows = f32[128,1024]{1,0:T(8,128)} all-gather(f32[8,1024]{1,0:T(8,128)S(1)} %reshape.43), channel_id=1, replica_groups={{0,1,2,3,4,5,6,7,8,9,10,11,12,13,14,15},{16,17,18,19,20,21,22,23,24,25,..., dimensions={0}, use_global_device_ids=true | all-gather | bytes 557056 | tf_op jit(solution)/shard_map/all_gather | solution.py:211
  33.1 9.8 %shard_map.56 = f32[768,1024]{1,0:T(8,128)} custom-call(s32[1,1]{1,0:T(1,128)S(6)} %copy.10.count, s32[1,1]{1,0:T(1,128)} %bitcast.10.base, f32[128,1024]{1,0:T(8,128)} %all_gather.6.rows, s32[1,256]{1,0:T(1,128)} %bitcast.25, s32[1,256]{1,0:T(1,128)} %bitcast.27, f32[64,64,256]{2,1,0:T(8,128)} %bitcast.23), custom_call_target="tpu_custom_call" | custom-call | flops 10000000000 | bytes 8388608 | tf_op jit(solution)/shard_map/pallas_call | solution.py:182
  43.0 0.0 reduce-scatter.2.cloned.1.call-update
  43.0 0.8 dynamic-slice_bitcast_fusion
  43.9 27.6 %all_gather.7.refs_0_ = f32[192,1024]{1,0:T(8,128)S(1)} all-gather(f32[16,1024]{1,0:T(8,128)S(1)} %dynamic-slice_bitcast_fusion), channel_id=1, replica_groups={{0,64,128,192,256,320,384,448,512,576,640,704},{8,72,136,200,264,328,39..., dimensions={0}, use_global_device_ids=true | all-gather | bytes 851968 | tf_op jit(solution)/shard_map/all_gather | solution.py:220
  71.5 0.0 copy-start
  71.5 0.1 fusion.3
  71.5 4.3 %collective-permute-start.3 = (f32[96,1024]{1,0:T(8,128)S(1)}, f32[96,1024]{1,0:T(8,128)S(1)}, u32[]{:S(2)}, u32[]{:S(2)}) collective-permute-start(f32[96,1024]{1,0:T(8,128)S(1)} %get-tuple-element.13), channel_id=1, source_target_pairs={{0,48},{8,56},{16,0},{24,8},{32,16},{40,24},{48,32},{56,40},{64,11... | collective-permute-start | bytes 1179656 | tf_op jit(solution)/shard_map/ppermute | solution.py:229
  75.9 1.9 %collective-permute-start = (f32[96,1024]{1,0:T(8,128)S(1)}, f32[96,1024]{1,0:T(8,128)S(1)}, u32[]{:S(2)}, u32[]{:S(2)}) collective-permute-start(f32[96,1024]{1,0:T(8,128)S(1)} %get-tuple-element.14), channel_id=1, source_target_pairs={{0,16},{8,24},{16,32},{24,40},{32,48},{40,56},{48,0},{56,8},{64,80... | collective-permute-start | bytes 1179656 | tf_op jit(solution)/shard_map/ppermute | solution.py:228
  77.8 2.1 %collective-permute-start.1 = (f32[96,1024]{1,0:T(8,128)S(1)}, f32[96,1024]{1,0:T(8,128)S(1)}, u32[]{:S(2)}, u32[]{:S(2)}) collective-permute-start(f32[96,1024]{1,0:T(8,128)S(1)} %get-tuple-element.13), channel_id=1, source_target_pairs={{0,16},{8,24},{16,32},{24,40},{32,48},{40,56},{48,0},{56,8},{64,80... | collective-permute-start | bytes 1179656 | tf_op jit(solution)/shard_map/ppermute | solution.py:230
  79.9 4.4 %collective-permute-start.5 = (f32[96,1024]{1,0:T(8,128)S(1)}, f32[96,1024]{1,0:T(8,128)S(1)}, u32[]{:S(2)}, u32[]{:S(2)}) collective-permute-start(f32[96,1024]{1,0:T(8,128)S(1)} %get-tuple-element.14), channel_id=1, source_target_pairs={{0,48},{8,56},{16,0},{24,8},{32,16},{40,24},{48,32},{56,40},{64,11... | collective-permute-start | bytes 1179656 | tf_op jit(solution)/shard_map/ppermute | solution.py:231
  84.3 0.0 collective-permute-done.3.refs_6_
  84.3 0.0 copy-start.1
  84.3 3.4 %collective-permute-start.4 = (f32[96,1024]{1,0:T(8,128)S(1)}, f32[96,1024]{1,0:T(8,128)S(1)}, u32[]{:S(2)}, u32[]{:S(2)}) collective-permute-start(f32[96,1024]{1,0:T(8,128)S(1)} %collective-permute-done.3.refs_6_), channel_id=1, source_target_pairs={{0,48},{8,56},{16,0},{24,8},{32,16},{40,24},{48,32},{56,40},{64,11... | collective-permute-start | bytes 1179656 | tf_op jit(solution)/shard_map/ppermute | solution.py:233
  87.7 0.0 collective-permute-done.refs_1_
  87.7 0.0 copy-start.2
  87.7 2.1 %collective-permute-start.2 = (f32[96,1024]{1,0:T(8,128)S(1)}, f32[96,1024]{1,0:T(8,128)S(1)}, u32[]{:S(2)}, u32[]{:S(2)}) collective-permute-start(f32[96,1024]{1,0:T(8,128)S(1)} %collective-permute-done.refs_1_), channel_id=1, source_target_pairs={{0,16},{8,24},{16,32},{24,40},{32,48},{40,56},{48,0},{56,8},{64,80... | collective-permute-start | bytes 1179656 | tf_op jit(solution)/shard_map/ppermute | solution.py:232
  89.8 0.5 collective-permute-done.1.refs_2_
  90.4 0.0 copy-start.3
  90.4 2.6 %collective-permute-done.5.refs_5_ = f32[96,1024]{1,0:T(8,128)S(1)} collective-permute-done((f32[96,1024]{1,0:T(8,128)S(1)}, f32[96,1024]{1,0:T(8,128)S(1)}, u32[]{:S(2)}, u32[]{:S(2)}) %collective-permute-start.5) | collective-permute-done | bytes 393248 | tf_op jit(solution)/shard_map/ppermute | solution.py:231
  92.9 0.0 copy-start.4
  93.0 7.5 %collective-permute-done.4.refs_4_ = f32[96,1024]{1,0:T(8,128)S(1)} collective-permute-done((f32[96,1024]{1,0:T(8,128)S(1)}, f32[96,1024]{1,0:T(8,128)S(1)}, u32[]{:S(2)}, u32[]{:S(2)}) %collective-permute-start.4) | collective-permute-done | bytes 393248 | tf_op jit(solution)/shard_map/ppermute | solution.py:233
  100.5 1.5 collective-permute-done.2.refs_3_
  102.0 0.0 copy-done
  102.0 0.0 copy-done.1
  102.0 0.0 copy-done.2
  102.0 0.0 copy-done.3
  102.0 0.0 copy-done.4
  102.1 0.0 copy-done.5
  102.1 0.7 copy-done.6
  102.8 10.9 %shard_map.55 = (f32[32,1024]{1,0:T(8,128)}, f32[32,1024]{1,0:T(8,128)}) custom-call(s32[1,1]{1,0:T(1,128)S(6)} %copy.10.count, s32[1,1]{1,0:T(1,128)} %bitcast.row, s32[1,1]{1,0:T(1,128)} %bitcast.1.col, f32[192,1024]{1,0:T(8,128)} %copy-done, f32[96,1024]{1,0:T(8,128)} %copy-done.2, f32[96,1024]{1,0:T(8,128)} %copy-done.3, f32[96,1024]{1,0:T(8,128)} %copy-done.6, ...), custom_call_target="tpu_custom_call" | custom-call | flops 10000000000 | bytes 8388608 | tf_op jit(solution)/shard_map/pallas_call | solution.py:182
  113.7 0.0 reduce-scatter.2.cloned.1.call-done
  113.7 8.5 %all-to-all-start = ((f32[8,8,1024]{2,1,0:T(8,128)}), f32[8,8,1024]{2,1,0:T(8,128)S(1)}, u32[]{:S(2)}, u32[]{:S(2)}) async-start(f32[8,8,1024]{2,1,0:T(8,128)} %bitcast.19), calls=%async_computation.1 | async-start | bytes 524288 | tf_op jit(solution)/shard_map/all_to_all | solution.py:247
  122.3 7.7 %collective-permute-start.6 = (f32[32,1024]{1,0:T(8,128)}, f32[32,1024]{1,0:T(8,128)S(1)}, u32[]{:S(2)}, u32[]{:S(2)}) collective-permute-start(f32[32,1024]{1,0:T(8,128)} %get-tuple-element.12), channel_id=1, source_target_pairs={{0,1},{1,0},{2,3},{3,2},{4,5},{5,4},{6,7},{7,6},{8,9},{9,8},{10,11... | collective-permute-start | bytes 393224 | tf_op jit(solution)/shard_map/ppermute | solution.py:250
  130.0 1.2 collective-permute-done.6
  131.2 0.9 add.21
  132.1 5.1 %collective-permute-start.7 = (f32[8,1024]{1,0:T(8,128)S(1)}, f32[8,1024]{1,0:T(8,128)S(1)}, u32[]{:S(2)}, u32[]{:S(2)}) collective-permute-start(f32[8,1024]{1,0:T(8,128)S(1)} %get-tuple-element.15), channel_id=1, source_target_pairs={{0,2},{1,3},{2,4},{3,5},{4,6},{5,7},{6,0},{7,1},{8,10},{9,11},{10,... | collective-permute-start | bytes 98312 | tf_op jit(solution)/shard_map/ppermute | solution.py:254
  137.2 1.9 %collective-permute-start.9 = (f32[8,1024]{1,0:T(8,128)S(1)}, f32[8,1024]{1,0:T(8,128)S(1)}, u32[]{:S(2)}, u32[]{:S(2)}) collective-permute-start(f32[8,1024]{1,0:T(8,128)S(1)} %get-tuple-element.16), channel_id=1, source_target_pairs={{0,6},{1,7},{2,0},{3,1},{4,2},{5,3},{6,4},{7,5},{8,14},{9,15},{10,... | collective-permute-start | bytes 98312 | tf_op jit(solution)/shard_map/ppermute | solution.py:254
  139.2 2.2 %collective-permute-start.8 = (f32[8,1024]{1,0:T(8,128)S(1)}, f32[8,1024]{1,0:T(8,128)S(1)}, u32[]{:S(2)}, u32[]{:S(2)}) collective-permute-start(f32[8,1024]{1,0:T(8,128)S(1)} %get-tuple-element.17), channel_id=1, source_target_pairs={{0,4},{1,5},{2,6},{3,7},{4,0},{5,1},{6,2},{7,3},{8,12},{9,13},{10,... | collective-permute-start | bytes 98312 | tf_op jit(solution)/shard_map/ppermute | solution.py:254
  141.4 0.0 all-to-all-done
  141.4 0.0 collective-permute-done.7
  141.4 2.3 %collective-permute-done.9 = f32[8,1024]{1,0:T(8,128)S(1)} collective-permute-done((f32[8,1024]{1,0:T(8,128)S(1)}, f32[8,1024]{1,0:T(8,128)S(1)}, u32[]{:S(2)}, u32[]{:S(2)}) %collective-permute-start.9) | collective-permute-done | bytes 32800 | tf_op jit(solution)/shard_map/ppermute | solution.py:254
  143.7 1.4 collective-permute-done.8
  145.1 0.1 reshape.47
  145.2 0.7 reshape.48
  (7 shorter events, 0.1 us)
Async XLA Ops:
  6.5 107.2 %reduce-scatter.2.cloned.1.call-start = ((), (), s32[]{:S(2)}) async-start(), calls=%async_computation.2 | async-start | bytes 3407872 | tf_op jit(solution)/shard_map/reduce_scatter | solution.py:216
  71.5 30.6 %copy-start = (f32[192,1024]{1,0:T(8,128)}, f32[192,1024]{1,0:T(8,128)S(1)}, u32[]{:S(2)}) copy-start(f32[192,1024]{1,0:T(8,128)S(1)} %all_gather.7.refs_0_) | copy-start | bytes 2359300
  71.5 12.8 %collective-permute-start.3 = (f32[96,1024]{1,0:T(8,128)S(1)}, f32[96,1024]{1,0:T(8,128)S(1)}, u32[]{:S(2)}, u32[]{:S(2)}) collective-permute-start(f32[96,1024]{1,0:T(8,128)S(1)} %get-tuple-element.13), channel_id=1, source_target_pairs={{0,48},{8,56},{16,0},{24,8},{32,16},{40,24},{48,32},{56,40},{64,11... | collective-permute-start | bytes 1179656 | tf_op jit(solution)/shard_map/ppermute | solution.py:229
  75.9 11.8 %collective-permute-start = (f32[96,1024]{1,0:T(8,128)S(1)}, f32[96,1024]{1,0:T(8,128)S(1)}, u32[]{:S(2)}, u32[]{:S(2)}) collective-permute-start(f32[96,1024]{1,0:T(8,128)S(1)} %get-tuple-element.14), channel_id=1, source_target_pairs={{0,16},{8,24},{16,32},{24,40},{32,48},{40,56},{48,0},{56,8},{64,80... | collective-permute-start | bytes 1179656 | tf_op jit(solution)/shard_map/ppermute | solution.py:228
  77.8 12.6 %collective-permute-start.1 = (f32[96,1024]{1,0:T(8,128)S(1)}, f32[96,1024]{1,0:T(8,128)S(1)}, u32[]{:S(2)}, u32[]{:S(2)}) collective-permute-start(f32[96,1024]{1,0:T(8,128)S(1)} %get-tuple-element.13), channel_id=1, source_target_pairs={{0,16},{8,24},{16,32},{24,40},{32,48},{40,56},{48,0},{56,8},{64,80... | collective-permute-start | bytes 1179656 | tf_op jit(solution)/shard_map/ppermute | solution.py:230
  79.9 13.0 %collective-permute-start.5 = (f32[96,1024]{1,0:T(8,128)S(1)}, f32[96,1024]{1,0:T(8,128)S(1)}, u32[]{:S(2)}, u32[]{:S(2)}) collective-permute-start(f32[96,1024]{1,0:T(8,128)S(1)} %get-tuple-element.14), channel_id=1, source_target_pairs={{0,48},{8,56},{16,0},{24,8},{32,16},{40,24},{48,32},{56,40},{64,11... | collective-permute-start | bytes 1179656 | tf_op jit(solution)/shard_map/ppermute | solution.py:231
  84.3 17.7 %copy-start.1 = (f32[96,1024]{1,0:T(8,128)}, f32[96,1024]{1,0:T(8,128)S(1)}, u32[]{:S(2)}) copy-start(f32[96,1024]{1,0:T(8,128)S(1)} %collective-permute-done.3.refs_6_) | copy-start | bytes 1179652
  84.3 16.2 %collective-permute-start.4 = (f32[96,1024]{1,0:T(8,128)S(1)}, f32[96,1024]{1,0:T(8,128)S(1)}, u32[]{:S(2)}, u32[]{:S(2)}) collective-permute-start(f32[96,1024]{1,0:T(8,128)S(1)} %collective-permute-done.3.refs_6_), channel_id=1, source_target_pairs={{0,48},{8,56},{16,0},{24,8},{32,16},{40,24},{48,32},{56,40},{64,11... | collective-permute-start | bytes 1179656 | tf_op jit(solution)/shard_map/ppermute | solution.py:233
  87.7 14.3 %copy-start.2 = (f32[96,1024]{1,0:T(8,128)}, f32[96,1024]{1,0:T(8,128)S(1)}, u32[]{:S(2)}) copy-start(f32[96,1024]{1,0:T(8,128)S(1)} %collective-permute-done.refs_1_) | copy-start | bytes 1179652
  87.7 14.3 %collective-permute-start.2 = (f32[96,1024]{1,0:T(8,128)S(1)}, f32[96,1024]{1,0:T(8,128)S(1)}, u32[]{:S(2)}, u32[]{:S(2)}) collective-permute-start(f32[96,1024]{1,0:T(8,128)S(1)} %collective-permute-done.refs_1_), channel_id=1, source_target_pairs={{0,16},{8,24},{16,32},{24,40},{32,48},{40,56},{48,0},{56,8},{64,80... | collective-permute-start | bytes 1179656 | tf_op jit(solution)/shard_map/ppermute | solution.py:232
  90.4 11.7 %copy-start.3 = (f32[96,1024]{1,0:T(8,128)}, f32[96,1024]{1,0:T(8,128)S(1)}, u32[]{:S(2)}) copy-start(f32[96,1024]{1,0:T(8,128)S(1)} %collective-permute-done.1.refs_2_) | copy-start | bytes 1179652
  92.9 9.1 %copy-start.4 = (f32[96,1024]{1,0:T(8,128)}, f32[96,1024]{1,0:T(8,128)S(1)}, u32[]{:S(2)}) copy-start(f32[96,1024]{1,0:T(8,128)S(1)} %collective-permute-done.5.refs_5_) | copy-start | bytes 1179652
  100.5 1.6 %copy-start.5 = (f32[96,1024]{1,0:T(8,128)}, f32[96,1024]{1,0:T(8,128)S(1)}, u32[]{:S(2)}) copy-start(f32[96,1024]{1,0:T(8,128)S(1)} %collective-permute-done.4.refs_4_) | copy-start | bytes 1179652
  102.0 0.7 copy-start.6
  113.7 27.6 %all-to-all-start = ((f32[8,8,1024]{2,1,0:T(8,128)}), f32[8,8,1024]{2,1,0:T(8,128)S(1)}, u32[]{:S(2)}, u32[]{:S(2)}) async-start(f32[8,8,1024]{2,1,0:T(8,128)} %bitcast.19), calls=%async_computation.1 | async-start | bytes 524288 | tf_op jit(solution)/shard_map/all_to_all | solution.py:247
  122.3 8.9 %collective-permute-start.6 = (f32[32,1024]{1,0:T(8,128)}, f32[32,1024]{1,0:T(8,128)S(1)}, u32[]{:S(2)}, u32[]{:S(2)}) collective-permute-start(f32[32,1024]{1,0:T(8,128)} %get-tuple-element.12), channel_id=1, source_target_pairs={{0,1},{1,0},{2,3},{3,2},{4,5},{5,4},{6,7},{7,6},{8,9},{9,8},{10,11... | collective-permute-start | bytes 393224 | tf_op jit(solution)/shard_map/ppermute | solution.py:250
  132.1 9.3 %collective-permute-start.7 = (f32[8,1024]{1,0:T(8,128)S(1)}, f32[8,1024]{1,0:T(8,128)S(1)}, u32[]{:S(2)}, u32[]{:S(2)}) collective-permute-start(f32[8,1024]{1,0:T(8,128)S(1)} %get-tuple-element.15), channel_id=1, source_target_pairs={{0,2},{1,3},{2,4},{3,5},{4,6},{5,7},{6,0},{7,1},{8,10},{9,11},{10,... | collective-permute-start | bytes 98312 | tf_op jit(solution)/shard_map/ppermute | solution.py:254
  137.2 6.5 %collective-permute-start.9 = (f32[8,1024]{1,0:T(8,128)S(1)}, f32[8,1024]{1,0:T(8,128)S(1)}, u32[]{:S(2)}, u32[]{:S(2)}) collective-permute-start(f32[8,1024]{1,0:T(8,128)S(1)} %get-tuple-element.16), channel_id=1, source_target_pairs={{0,6},{1,7},{2,0},{3,1},{4,2},{5,3},{6,4},{7,5},{8,14},{9,15},{10,... | collective-permute-start | bytes 98312 | tf_op jit(solution)/shard_map/ppermute | solution.py:254
  139.2 5.9 %collective-permute-start.8 = (f32[8,1024]{1,0:T(8,128)S(1)}, f32[8,1024]{1,0:T(8,128)S(1)}, u32[]{:S(2)}, u32[]{:S(2)}) collective-permute-start(f32[8,1024]{1,0:T(8,128)S(1)} %get-tuple-element.17), channel_id=1, source_target_pairs={{0,4},{1,5},{2,6},{3,7},{4,0},{5,1},{6,2},{7,3},{8,12},{9,13},{10,... | collective-permute-start | bytes 98312 | tf_op jit(solution)/shard_map/ppermute | solution.py:254
Sparse Core Ops, SparseCore 0:
  43.1 58.1 reduce-scatter.1
